TPU v7x, 32 devices: a whole 2x2x4 slice. The times are simulated.
32 devices in a mesh: grp: 8 (over y, x, core), band: 4 (over z).
Axes of the slice: x: 2, y: 2, z: 4, core: 2. Of those that a mesh axis runs over, the one named last changes fastest.
Arguments:
- voltages: bfloat16 [64, 2048, 2048], P('band', 'grp'), may hold values from -6 to 6
- steering: int32 [2, 1024], replicated, may hold values from 0 to 255, as said below
- chan_sub: int32 [1024], P('band'), may hold values from 0 to 15, as said below
- delays: int32 [512, 16], P(None, 'band'), may hold values from 0 to 63
Outputs:
- dedispersed: float32 [64, 1024, 512], P(None, 'grp', 'band')
Inputs may be any that keep to these rules, and one draw needn't show every extreme that they name: Every pair (steering[0, b], steering[1, b]) with the first below 256 and the second below 4 occurs for exactly one beam b. chan_sub[c] // 4 == c // 256: a channel belongs to a subband of its own quarter of the band.
All inputs are finite; a program needn't handle non-finite values.
Results may differ from a plain program's by a relative error of at most 0.0041.
Values may be sent and summed in bfloat16 or wider, within the bound.
A program may use at most 128 MiB of HBM per device.

v0:
```python
import math

import jax
import jax.numpy as jnp
from jax import lax
from jax.sharding import PartitionSpec as P

A = 2048
FEEDS = 1024
NS_FEEDS = 256
C = 1024
SAMP = 2048
BEAMS = 1024


def shifted(block, axis, distance):
    devices = range(lax.axis_size(axis))
    route = [(i - distance, i) for i in devices if i - distance in devices]
    return lax.ppermute(block, axis, route)


def window_taps():
    tap_pos = jnp.arange(4 * SAMP, dtype=jnp.float32) + 0.5
    hann_taper = 0.5 - 0.5 * jnp.cos(2.0 * math.pi / (4 * SAMP) * tap_pos)
    window = hann_taper * jnp.sinc((tap_pos - 2 * SAMP) / SAMP)
    window = window * jnp.sqrt(SAMP / jnp.sum(window * window))
    return window.reshape(4, SAMP)


def dft_table():
    row_ids = jnp.arange(SAMP, dtype=jnp.int32)
    col_ids = jnp.arange(SAMP, dtype=jnp.int32)
    chan_ids = row_ids % C
    phase_steps = chan_ids[:, None] * col_ids[None, :] % SAMP
    angles = 2.0 * math.pi / SAMP * phase_steps.astype(jnp.float32)
    row_scale = 1.0 / math.sqrt(SAMP)
    table = jnp.where((row_ids < C)[:, None], jnp.cos(angles), -jnp.sin(angles)) * row_scale
    return table.astype(jnp.bfloat16)


def beam_weights(channel_at, steering):
    feed_ids = jnp.arange(FEEDS, dtype=jnp.int32)
    north_pos = (feed_ids % NS_FEEDS).astype(jnp.float32) / NS_FEEDS
    east_pos = (feed_ids // NS_FEEDS).astype(jnp.float32) / 4.0
    geometry = north_pos[:, None] * steering[0][None, :].astype(jnp.float32) + east_pos[
        :, None
    ] * steering[1][None, :].astype(jnp.float32)
    frequency = 1.0 - channel_at.astype(jnp.float32) / (2 * C)
    phases = 2.0 * math.pi * frequency * geometry
    weight_norm = 1.0 / math.sqrt(FEEDS)
    return jnp.concatenate(
        [jnp.cos(phases) * weight_norm, jnp.sin(phases) * weight_norm], axis=1
    ).astype(jnp.bfloat16)


def intensity(channel_block, weights):
    frames = channel_block.shape[1]
    input_rows = channel_block.reshape(4 * frames, FEEDS)
    products = jnp.dot(input_rows, weights, preferred_element_type=jnp.float32).reshape(
        2, frames, 2, 2, BEAMS
    )
    beam_re = products[0, :, :, 0] - products[1, :, :, 1]
    beam_im = products[0, :, :, 1] + products[1, :, :, 0]
    return jnp.sum(beam_re * beam_re + beam_im * beam_im, axis=1).astype(jnp.bfloat16)


def channel_power(turned, first_channel, steering):

    def one_channel(channel_at):
        channel_block = lax.dynamic_index_in_dim(turned, channel_at, 1, keepdims=False)
        return intensity(channel_block, beam_weights(first_channel + channel_at, steering))

    return lax.map(one_channel, jnp.arange(turned.shape[1], dtype=jnp.int32))


def fourier_tables(total_frames):
    half_frames = total_frames // 2
    freq_ids = jnp.arange(1, half_frames + 1, dtype=jnp.int32)
    time_ids = jnp.arange(total_frames, dtype=jnp.int32)
    angles = (
        2.0
        * math.pi
        / total_frames
        * (freq_ids[:, None] * time_ids[None, :] % total_frames).astype(jnp.float32)
    )
    cosines = jnp.cos(angles)
    sines = jnp.sin(angles)
    forward = jnp.concatenate([cosines, -sines], axis=0)
    weight = jnp.where(freq_ids == half_frames, 1.0, 2.0).astype(jnp.float32) / (
        total_frames * math.sqrt(C)
    )
    inverse = jnp.transpose(
        jnp.concatenate([cosines * weight[:, None], -sines * weight[:, None]], axis=0)
    )
    return (forward, inverse)


def trial_phases(delays, total_frames):
    freq_ids = jnp.arange(1, total_frames // 2 + 1, dtype=jnp.int32)
    phase_steps = freq_ids[:, None, None] * jnp.transpose(delays)[None, :, :] % total_frames
    angles = 2.0 * math.pi / total_frames * phase_steps.astype(jnp.float32)
    return (jnp.cos(angles), jnp.sin(angles))


def dedisperse(centered, delays, total_frames):
    highest = lax.Precision.HIGHEST
    forward, inverse = fourier_tables(total_frames)
    half_frames = total_frames // 2
    spectrum = jnp.einsum("km,smb->ksb", forward, centered, precision=highest)
    spec_re = spectrum[:half_frames]
    spec_im = spectrum[half_frames:]
    cosines, sines = trial_phases(delays, total_frames)
    shifted_re = jnp.einsum("ksb,ksd->kbd", spec_re, cosines, precision=highest) + jnp.einsum(
        "ksb,ksd->kbd", spec_im, sines, precision=highest
    )
    shifted_im = jnp.einsum("ksb,ksd->kbd", spec_im, cosines, precision=highest) - jnp.einsum(
        "ksb,ksd->kbd", spec_re, sines, precision=highest
    )
    stacked = jnp.concatenate([shifted_re, shifted_im], axis=0)
    beams_here = centered.shape[2]
    trials_all = delays.shape[0]
    flattened = jnp.dot(
        inverse,
        stacked.reshape(2 * half_frames, beams_here * trials_all),
        precision=highest,
        preferred_element_type=jnp.float32,
    )
    return flattened.reshape(total_frames, beams_here, trials_all)


def local(voltages, steering, chan_sub, delays):
    groups = lax.axis_size("grp")
    band_count = lax.axis_size("band")
    grp_at = lax.axis_index("grp")
    band_at = lax.axis_index("band")
    local_frames, local_inputs, samples = voltages.shape
    total_frames = local_frames * band_count
    local_beams = BEAMS // groups
    rim_rows = shifted(voltages[local_frames - 3 :], "band", 1)
    padded = jnp.concatenate([rim_rows, voltages], axis=0)
    window = window_taps()
    filtered = window[0][None, None, :] * padded[0:local_frames].astype(jnp.float32)
    for tap_at in range(1, 4):
        filtered = filtered + window[tap_at][None, None, :] * padded[
            tap_at : tap_at + local_frames
        ].astype(jnp.float32)
    filtered = filtered.astype(jnp.bfloat16).reshape(local_frames * local_inputs, samples)
    spectra = lax.dot_general(
        dft_table(), filtered, (((1,), (1,)), ((), ())), preferred_element_type=jnp.float32
    ).astype(jnp.bfloat16)
    per_dev = C // (groups * band_count)
    blocks = spectra.reshape(2, band_count, groups, per_dev, local_frames, local_inputs)
    turned = lax.all_to_all(
        lax.all_to_all(blocks, "grp", split_axis=2, concat_axis=5, tiled=True),
        "band",
        split_axis=1,
        concat_axis=4,
        tiled=True,
    )
    turned = turned.reshape(2, per_dev, total_frames, A)
    first_channel = band_at * (C // band_count) + grp_at * per_dev
    beam_power = channel_power(turned, first_channel, steering)
    split_beams = beam_power.reshape(per_dev, total_frames, groups, local_beams)
    quarter = lax.all_to_all(split_beams, "grp", split_axis=2, concat_axis=0, tiled=True)
    quarter_chans = quarter.shape[0]
    local_subs = delays.shape[1]
    sub_ids = band_at * local_subs + jnp.arange(local_subs, dtype=jnp.int32)
    member = (chan_sub[:, None] == sub_ids[None, :]).astype(jnp.bfloat16)
    band_sums = jnp.dot(
        jnp.transpose(member),
        quarter.reshape(quarter_chans, total_frames * local_beams),
        preferred_element_type=jnp.float32,
    )
    band_sums = band_sums.reshape(local_subs, total_frames, local_beams)
    centered = band_sums - jnp.mean(band_sums, axis=1, keepdims=True)
    own_delays = lax.all_to_all(delays, "band", split_axis=0, concat_axis=1, tiled=True)
    every_sub = lax.all_gather(centered, "band", axis=0, tiled=True)
    return dedisperse(every_sub, own_delays, total_frames)


def solution(mesh):
    in_specs = (P("band", "grp", None), P(), P("band"), P(None, "band"))
    out_specs = P(None, "grp", "band")
    return jax.shard_map(local, mesh=mesh, in_specs=in_specs, out_specs=out_specs, check_vma=False)
```

profile of v0, /device:TPU:0, one launch (start us, length us, event | category | flops | bytes accessed | tf_op | source)
XLA Modules:
  0.0 1803.9 jit_solution(14523196060346809055)
XLA Ops:
  10.9 71.8 %multiply_convert_fusion.6 = bf16[2048,2048]{1,0:T(8,128)(2,1)} fusion(s32[2048]{0:T(1024)S(1)} %add_select_fusion.5, pred[2048]{0:T(1024)(128)(4,1)S(1)} %iota_compare_fusion), kind=kLoop, calls=%fused_computation.35.clone.clone.1 | loop fusion | flops 75497472 | bytes 8398848 | tf_op jit(solution)/shard_map/dot_general | solution.py:148
  84.6 7.1 constant_dynamic-update-slice_fusion
  91.7 29.4 %add_convert_fusion = bf16[16,256,2048]{2,1,0:T(8,128)(2,1)} fusion(bf16[16,256,2048]{2,1,0:T(8,128)(2,1)} %param.6, bf16[19,256,2048]{2,1,0:T(8,128)(2,1)} %constant_dynamic-update-slice_fusion, f32[2048]{0:T(1024)S(1)} %get-tuple-element.128, f32[2048]{0:T(1024)S(1)} %get-tuple-element.129, f32[2048]{0:T(1024)S(1)} %get-tuple-element.130, ...), kind=kLoop, calls=%fused_computation.28 | loop fusion | flops 100663296 | bytes 83918848 | tf_op jit(solution)/shard_map/convert_element_type | solution.py:147
  121.1 40.6 %convolution_convert_fusion = bf16[2048,4096]{1,0:T(8,128)(2,1)S(1)} fusion(bf16[4096,2048]{1,0:T(8,128)(2,1)} %bitcast.112, bf16[2048,2048]{1,0:T(8,128)(2,1)} %multiply_convert_fusion.6), kind=kOutput, calls=%fused_computation.39 | convolution fusion | flops 34368126976 | bytes 41943040 | tf_op jit(solution)/shard_map/dot_general | solution.py:148
  168.5 187.6 %all_to_all.67 = bf16[2,4,8,32,16,256]{5,4,3,1,0,2:T(8,128)(2,1)S(1)} all-to-all(bf16[2,4,8,32,16,256]{5,4,3,1,0,2:T(8,128)(2,1)S(1)} %copy.42), channel_id=1, replica_groups=mesh['grp'=8,'band'=4] {'grp'}, dimensions={2} | all-to-all | bytes 33554432 | tf_op jit(solution)/shard_map/all_to_all | solution.py:154
  356.1 15.2 copy.64
  371.3 25.6 %reshape.141 = bf16[2,4,1,32,16,2048]{5,4,3,0,2,1:T(8,128)(2,1)} reshape(bf16[2,4,1,32,16,8,256]{6,5,4,3,0,1,2:T(8,128)(2,1)} %copy.64) | data formatting | bytes 33554432 | tf_op jit(solution)/shard_map/all_to_all | solution.py:154
  396.9 7.1 all-to-all-start.1
  404.1 362.4 %all-to-all-done.1 = bf16[2,4,1,32,16,2048]{5,4,3,0,2,1:T(8,128)(2,1)} async-done(((bf16[2,4,1,32,16,2048]{5,4,3,0,2,1:T(8,128)(2,1)}), bf16[2,4,1,32,16,2048]{5,4,3,0,2,1:T(8,128)(2,1)}, u32[]{:S(2)}, u32[]{:S(2)}) %all-to-all-start.1) | async-done | bytes 16777248 | tf_op jit(solution)/shard_map/all_to_all | solution.py:153
  766.5 14.1 copy.45
  780.5 892.0 %while.12 = (s32[]{:T(128)}, bf16[32,64,1024]{2,1,0:T(8,128)(2,1)}, s32[32]{0:T(128)S(1)}, bf16[2,32,64,2048]{3,2,1,0:T(8,128)(2,1)}, s32[]{:T(128)}, /*index=5*...) while((s32[]{:T(128)}, bf16[32,64,1024]{2,1,0:T(8,128)(2,1)}, ...), condition=%wide.region_3.4_spmd, body=%wide.region_1.3_spmd.sunk | while | flops 1091256320 | bytes 24011500 | solution.py:73
  781.9 16.3 multiply_convert_fusion.8
  809.8 16.3 multiply_convert_fusion.8
  837.6 16.3 multiply_convert_fusion.8
  865.5 16.3 multiply_convert_fusion.8
  893.4 16.3 multiply_convert_fusion.8
  921.3 16.3 multiply_convert_fusion.8
  949.1 16.3 multiply_convert_fusion.8
  977.0 16.3 multiply_convert_fusion.8
  1004.9 16.3 multiply_convert_fusion.8
  1032.8 16.3 multiply_convert_fusion.8
  1060.6 16.3 multiply_convert_fusion.8
  1088.5 16.3 multiply_convert_fusion.8
  1116.4 16.3 multiply_convert_fusion.8
  1144.3 16.3 multiply_convert_fusion.8
  1172.1 16.3 multiply_convert_fusion.8
  1200.0 16.3 multiply_convert_fusion.8
  1227.9 16.3 multiply_convert_fusion.8
  1255.7 16.3 multiply_convert_fusion.8
  1283.6 16.3 multiply_convert_fusion.8
  1311.5 16.3 multiply_convert_fusion.8
  1339.4 16.3 multiply_convert_fusion.8
  1367.2 16.3 multiply_convert_fusion.8
  1395.1 16.3 multiply_convert_fusion.8
  1423.0 16.3 multiply_convert_fusion.8
  1450.9 16.3 multiply_convert_fusion.8
  1478.7 16.3 multiply_convert_fusion.8
  1506.6 16.3 multiply_convert_fusion.8
  1534.5 16.3 multiply_convert_fusion.8
  1562.4 16.3 multiply_convert_fusion.8
  1590.2 16.3 multiply_convert_fusion.8
  1618.1 16.3 multiply_convert_fusion.8
  1646.0 16.3 multiply_convert_fusion.8
  1682.6 48.9 %all-to-all-done.2 = bf16[32,64,8,128]{3,1,0,2:T(8,128)(2,1)} async-done(((bf16[32,64,8,128]{3,1,0,2:T(8,128)(2,1)}), bf16[32,64,8,128]{3,1,0,2:T(8,128)(2,1)}, u32[]{:S(2)}, u32[]{:S(2)}) %all-to-all-start.2) | async-done | bytes 4194336 | tf_op jit(solution)/shard_map/all_to_all | solution.py:164
  1735.2 12.3 copy.91
  1747.6 6.4 copy.48
  1757.4 16.7 all_gather.3
  1792.8 6.0 fusion.28
  (297 shorter events, 342.5 us)
Async XLA Ops:
  4.0 78.7 %collective-permute-start = (bf16[3,256,2048]{2,1,0:T(8,128)(2,1)}, bf16[3,256,2048]{2,1,0:T(8,128)(2,1)S(1)}, u32[]{:S(2)}, u32[]{:S(2)}) collective-permute-start(bf16[3,256,2048]{2,1,0:T(8,128)(2,1)} %slice.69), channel_id=1, source_target_pairs={{0,1},{1,2},{2,3},{4,5},{5,6},{6,7},{8,9},{9,10},{10,11},{12,13},{... | collective-permute-start | bytes 9437192 | tf_op jit(solution)/shard_map/ppermute | solution.py:19
  10.8 73.7 %copy-start = (bf16[16,256,2048]{2,1,0:T(8,128)(2,1)S(1)}, bf16[16,256,2048]{2,1,0:T(8,128)(2,1)}, u32[]{:S(2)}) copy-start(bf16[16,256,2048]{2,1,0:T(8,128)(2,1)} %param.6) | copy-start | bytes 50331652
  396.9 7.1 copy-start.1
  396.9 369.6 %all-to-all-start.1 = ((bf16[2,4,1,32,16,2048]{5,4,3,0,2,1:T(8,128)(2,1)}), bf16[2,4,1,32,16,2048]{5,4,3,0,2,1:T(8,128)(2,1)}, u32[]{:S(2)}, u32[]{:S(2)}) async-start(bf16[2,4,1,32,16,2048]{5,4,3,0,2,1:T(8,128)(2,1)} %reshape.141), calls=%async_computation.1 | async-start | bytes 33554432 | tf_op jit(solution)/shard_map/all_to_all | solution.py:153
  1677.9 53.7 %all-to-all-start.2 = ((bf16[32,64,8,128]{3,1,0,2:T(8,128)(2,1)}), bf16[32,64,8,128]{3,1,0,2:T(8,128)(2,1)}, u32[]{:S(2)}, u32[]{:S(2)}) async-start(bf16[32,64,8,128]{3,1,0,2:T(8,128)(2,1)} %copy_bitcast_fusion), calls=%async_computation.2 | async-start | bytes 8388608 | tf_op jit(solution)/shard_map/all_to_all | solution.py:164
  1731.6 43.1 %all-to-all-start.3 = ((s32[4,128,4]{1,2,0:T(4,128)}), s32[4,128,4]{1,2,0:T(4,128)S(1)}, u32[]{:S(2)}, u32[]{:S(2)}) async-start(s32[4,128,4]{1,2,0:T(4,128)} %bitcast.22), calls=%async_computation.3 | async-start | bytes 16384 | tf_op jit(solution)/shard_map/all_to_all | solution.py:176
  1747.6 6.4 copy-start.2
where the time goes:
time: 1820 us; the launch traced here: 1800 us
  other arithmetic  707 us (39%)
  waiting for transfers between devices  411 us (23%)
  blocking collectives  204 us (11%)
  local copies, waits for them, and re-layouts  192 us (11%)
  matrix products  179 us (10%)
  loops' own time  88.1 us (5%)
  starting transfers between devices  20.4 us (1%)
    another operation x32, other arithmetic  521 us
    all_to_all x1, waiting for transfers between devices, local(): lax.all_to_all(lax.all_to_all(blocks, 'grp', split_axis=2, concat_axis=5,...  362 us
    all_to_all x1, blocking collectives, local(): lax.all_to_all(blocks, 'grp', split_axis=2, concat_axis=5, tiled=True)  188 us
    dot_general x32, matrix products, intensity(): jnp.dot(input_rows, weights, preferred_element_type=jnp.float32)  111 us
    another operation x1, loops' own time, channel_power(): return lax.map(one_channel, jnp.arange(turned.shape[1], dtype=jnp.int32))  88.1 us
    concatenate x32, other arithmetic, beam_weights(): jnp.concatenate([jnp.cos(phases) * weight_norm, jnp.sin(phases) * weight_...  76.2 us
    dot_general x1, other arithmetic, local(): lax.dot_general(dft_table(), filtered, (((1,), (1,)), ((), ())), preferre...  71.8 us
    all_to_all x1, waiting for transfers between devices, local(): lax.all_to_all(split_beams, 'grp', split_axis=2, concat_axis=0, tiled=True)  48.9 us
  transfers between devices with their start and end apart: 4, of which 2 were waited for; matrix products, arithmetic and copies ran while one was open for 5% of the time, Pallas kernels for 0%

commit v1 on v0

v1 whole, which is shorter than its diff:
```python
import math

import jax
import jax.numpy as jnp
from jax import lax
from jax.sharding import PartitionSpec as P

A = 2048
FEEDS = 1024
NS_FEEDS = 256
EW_FEEDS = 4
C = 1024
SAMP = 2048
BEAMS = 1024
QUARTERS = 4
POLS = 2
GROUP_FRAMES = 4


def shifted(block, axis, distance):
    devices = range(lax.axis_size(axis))
    route = [(i - distance, i) for i in devices if i - distance in devices]
    return lax.ppermute(block, axis, route)


def window_taps():
    tap_pos = jnp.arange(4 * SAMP, dtype=jnp.float32) + 0.5
    hann_taper = 0.5 - 0.5 * jnp.cos(2.0 * math.pi / (4 * SAMP) * tap_pos)
    window = hann_taper * jnp.sinc((tap_pos - 2 * SAMP) / SAMP)
    window = window * jnp.sqrt(SAMP / jnp.sum(window * window))
    return window.reshape(4, SAMP)


def unit_circle(steps, whole):
    angles = 2.0 * math.pi / whole * (steps % whole).astype(jnp.float32)
    return (jnp.cos(angles), jnp.sin(angles))


def dft_rows(first_channel, count):
    low = 32
    col_ids = jnp.arange(SAMP, dtype=jnp.int32)[None, :]
    hi_ids = first_channel + low * jnp.arange(count // low, dtype=jnp.int32)
    lo_ids = jnp.arange(low, dtype=jnp.int32)
    hi_re, hi_im = unit_circle(hi_ids[:, None] * col_ids, SAMP)
    lo_re, lo_im = unit_circle(lo_ids[:, None] * col_ids, SAMP)
    hi_re, hi_im, lo_re, lo_im = lax.optimization_barrier((hi_re, hi_im, lo_re, lo_im))
    scale = 1.0 / math.sqrt(SAMP)
    real = (hi_re[:, None] * lo_re[None] - hi_im[:, None] * lo_im[None]) * scale
    imag = (hi_re[:, None] * lo_im[None] + hi_im[:, None] * lo_re[None]) * -scale
    return jnp.concatenate(
        [real.reshape(count, SAMP), imag.reshape(count, SAMP)], axis=0
    ).astype(jnp.bfloat16)


def beam_sums(block, member, first_channel, east_ids):
    per, _, _, frames, _ = block.shape
    ids = jnp.arange(NS_FEEDS, dtype=jnp.int32)
    outer = ids[:, None] * ids[None, :]
    whole = 2 * C * NS_FEEDS
    span, low = min(per, 32), 8
    lo_re, lo_im = unit_circle(-outer[None] * jnp.arange(low, dtype=jnp.int32)[:, None, None], whole)
    def add_chunk(chunk_at, total):
        start = chunk_at * span
        at = 2 * C - first_channel - start - low * jnp.arange(span // low, dtype=jnp.int32)
        hi_re, hi_im = unit_circle(outer[None] * at[:, None, None], whole)
        hi_re, hi_im = lax.optimization_barrier((hi_re, hi_im))
        w_re = hi_re[:, None] * lo_re[None] - hi_im[:, None] * lo_im[None]
        w_im = hi_re[:, None] * lo_im[None] + hi_im[:, None] * lo_re[None]
        weights = jnp.concatenate([w_re, w_im], axis=3).astype(jnp.bfloat16)
        weights = lax.optimization_barrier(weights.reshape(span, NS_FEEDS, 2 * NS_FEEDS))
        rows = lax.dynamic_slice_in_dim(block, start, span).reshape(span, EW_FEEDS * 2 * frames, NS_FEEDS)
        products = lax.dot_general(
            rows, weights, (((2,), (1,)), ((0,), (0,))), preferred_element_type=jnp.float32
        ).reshape(span, EW_FEEDS, 2, frames, 2 * NS_FEEDS)
        y_re = products[:, :, 0, :, :NS_FEEDS] - products[:, :, 1, :, NS_FEEDS:]
        y_im = products[:, :, 0, :, NS_FEEDS:] + products[:, :, 1, :, :NS_FEEDS]
        freqs = 2 * C - first_channel - start - jnp.arange(span, dtype=jnp.int32)
        powers = []
        for beam in range(EW_FEEDS):
            t_re, t_im = unit_circle(
                freqs[:, None] * (beam * east_ids)[None, :], 2 * C * EW_FEEDS
            )
            sum_re, sum_im = 0.0, 0.0
            for east in range(EW_FEEDS):
                c_re, c_im = t_re[:, east, None, None], t_im[:, east, None, None]
                sum_re = sum_re + (y_re[:, east] * c_re - y_im[:, east] * c_im)
                sum_im = sum_im + (y_re[:, east] * c_im + y_im[:, east] * c_re)
            powers.append(sum_re * sum_re + sum_im * sum_im)
        power = jnp.concatenate(powers, axis=2)
        return total + jnp.einsum(
            "cs,cfb->sfb", lax.dynamic_slice_in_dim(member, start, span), power, precision=lax.Precision.HIGHEST
        )

    zeros = jnp.zeros((member.shape[1], frames, BEAMS), jnp.float32)
    return lax.fori_loop(0, per // span, add_chunk, zeros)


def dedisperse(centered, delays):
    subs, total_frames, beams = centered.shape
    trials = delays.shape[0]
    frame_ids = jnp.arange(total_frames, dtype=jnp.int32)
    key = (frame_ids[None, :, None] + jnp.transpose(delays)[:, None, :]) % total_frames
    pick = (key[:, :, None, :] == frame_ids[None, None, :, None]).astype(jnp.float32)
    shares = jnp.einsum("smb,smtd->btd", centered, pick, precision=lax.Precision.HIGHEST)
    return jnp.transpose(shares, (1, 0, 2)) * (1.0 / math.sqrt(C))


def local(voltages, steering, chan_sub, delays):
    groups = lax.axis_size("grp")
    bands = lax.axis_size("band")
    grp_at = lax.axis_index("grp")
    frames, inputs, samples = voltages.shape
    local_beams = BEAMS // groups
    local_subs = delays.shape[1]
    part = groups // POLS
    per = C // part
    first_channel = grp_at % part * per
    place = grp_at % part

    rim_rows = shifted(voltages[frames - 3 :], "band", 1)
    trials = delays.shape[0] // bands
    quarter_chans = chan_sub.shape[0]
    lists = jnp.concatenate(
        [
            delays.reshape(bands, trials * local_subs),
            jnp.broadcast_to(chan_sub[None, :], (bands, quarter_chans)),
        ],
        axis=1,
    )
    lists = lax.all_to_all(lists, "band", split_axis=0, concat_axis=0, tiled=True)
    own_delays = lists[:, : trials * local_subs].reshape(bands, trials, local_subs)
    own_delays = jnp.transpose(own_delays, (1, 0, 2)).reshape(trials, bands * local_subs)
    every_chan_sub = lists[:, trials * local_subs :].reshape(C)
    window = window_taps()
    tables = [lax.optimization_barrier(dft_rows((place ^ hop) * per, per)) for hop in range(part)]

    def exchanged(first):
        if first >= 3:
            padded = voltages[first - 3 : first + GROUP_FRAMES]
        else:
            padded = jnp.concatenate([rim_rows, voltages[:GROUP_FRAMES]], axis=0)
        filtered = window[0][None, None, :] * padded[0:GROUP_FRAMES].astype(jnp.float32)
        for tap_at in range(1, 4):
            filtered = filtered + window[tap_at][None, None, :] * padded[
                tap_at : tap_at + GROUP_FRAMES
            ].astype(jnp.float32)
        filtered = lax.optimization_barrier(
            filtered.astype(jnp.bfloat16).reshape(GROUP_FRAMES * inputs, samples)
        )
        turned = []
        for hop in list(range(1, part)) + [0]:
            spectra = lax.dot_general(
                tables[hop], filtered, (((1,), (1,)), ((), ())), preferred_element_type=jnp.float32
            ).astype(jnp.bfloat16)
            if hop:
                spectra = lax.ppermute(spectra, "grp", [(i, i ^ hop) for i in range(groups)])
            turned.append(spectra.reshape(2, per, GROUP_FRAMES * inputs))
        turned = turned[-1:] + turned[:-1]
        pieces = NS_FEEDS // inputs
        if pieces == 1:
            return turned
        turned = jnp.stack(turned)[place ^ jnp.arange(part, dtype=jnp.int32)]
        turned = turned.reshape(EW_FEEDS, pieces, 2, per, GROUP_FRAMES, inputs)
        turned = jnp.transpose(turned, (0, 2, 3, 4, 1, 5))
        turned = turned.reshape(EW_FEEDS, 2, per, GROUP_FRAMES * NS_FEEDS)
        return [turned[east] for east in range(EW_FEEDS)]

    firsts = list(range(GROUP_FRAMES, frames, GROUP_FRAMES)) + [0]
    turned = {first: exchanged(first) for first in firsts}
    received = [block for first in sorted(firsts) for block in turned[first]]
    east_ids = jnp.arange(EW_FEEDS, dtype=jnp.int32)
    if inputs == NS_FEEDS:
        east_ids = place ^ east_ids

    subs = lax.dynamic_slice_in_dim(every_chan_sub, first_channel, per) % local_subs
    member = (subs[:, None] == jnp.arange(local_subs, dtype=jnp.int32)[None, :]).astype(jnp.float32)
    groups_of = frames // GROUP_FRAMES
    block = jnp.stack(received).reshape(
        groups_of, EW_FEEDS, 2, per, GROUP_FRAMES, NS_FEEDS
    )
    block = jnp.transpose(block, (3, 1, 2, 0, 4, 5)).reshape(
        per, EW_FEEDS, 2, frames, NS_FEEDS
    )
    sums = beam_sums(block, member, first_channel, east_ids)
    grid_ids = jnp.arange(BEAMS, dtype=jnp.int32)
    beam_place = steering[1] * NS_FEEDS + steering[0]
    pick = (grid_ids[:, None] == beam_place[None, :]).astype(jnp.float32)
    ordered = jnp.dot(
        sums.reshape(local_subs * frames, BEAMS),
        pick,
        precision=lax.Precision.HIGHEST,
        preferred_element_type=jnp.float32,
    ) * (1.0 / FEEDS)
    by_owner = lax.all_to_all(
        ordered.reshape(local_subs, frames, groups, local_beams),
        "grp",
        split_axis=2,
        concat_axis=0,
    )
    own_sums = jnp.sum(
        by_owner.reshape(
            POLS, QUARTERS, part // QUARTERS, local_subs, frames, local_beams
        ),
        axis=(0, 2),
    ).reshape(QUARTERS * local_subs, frames, local_beams)
    every_frame = lax.all_gather(own_sums, "band", axis=0, tiled=True)
    every_frame = every_frame.reshape(bands, -1, frames, local_beams)
    every_frame = jnp.transpose(every_frame, (1, 0, 2, 3)).reshape(-1, bands * frames, local_beams)
    centered = every_frame - jnp.mean(every_frame, axis=1, keepdims=True)
    return dedisperse(centered, own_delays)


def solution(mesh):
    in_specs = (P("band", "grp", None), P(), P("band"), P(None, "band"))
    out_specs = P(None, "grp", "band")
    return jax.shard_map(local, mesh=mesh, in_specs=in_specs, out_specs=out_specs, check_vma=False)
```

time: 1820 us -> 737 us (0.40)
  other arithmetic: 707 us -> 297 us
  waiting for transfers between devices: 411 us -> 137 us
  blocking collectives: 204 us -> 15.7 us
  loops' own time: 88.1 us -> 19.2 us
  matrix products: 179 us -> 111 us
  local copies, waits for them, and re-layouts: 192 us -> 126 us
    another operation x32 -> x12, other arithmetic: 521 us -> 39 us
    all_to_all x3 -> x2, waiting for transfers between devices: 411 us -> 6.64 us  [the longest x1 6.64 us: local(): lax.all_to_all(ordered.reshape(local_subs, frames, groups, local_beams),...]
    all_to_all x1 -> x0, blocking collectives: 188 us -> none  [local(): lax.all_to_all(blocks, 'grp', split_axis=2, concat_axis=5, tiled=True)]
    ppermute x0 -> x12, waiting for transfers between devices: none -> 130 us  [exchanged(): lax.ppermute(spectra, 'grp', [(i, i ^ hop) for i in range(groups)])]
    dot_general x1 -> x0, other arithmetic: 71.8 us -> none  [local(): lax.dot_general(dft_table(), filtered, (((1,), (1,)), ((), ())), preferre...]
    add x2 -> x45, other arithmetic: 0.01 us -> 71.5 us  [the longest x8 51.5 us: add_chunk(): y_im = products[:, :, 0, :, NS_FEEDS:] + products[:, :, 1, :, :NS_FEEDS]]
    another operation x1, loops' own time: 88.1 us -> 19.2 us  [beam_sums(): return lax.fori_loop(0, per // span, add_chunk, zeros)]
    dot_general x40 -> x34, matrix products: 179 us -> 111 us  [the longest x16 47.7 us: exchanged(): lax.dot_general(tables[hop], filtered, (((1,), (1,)), ((), ())), preferre...]
  transfers between devices with their start and end apart: 4 -> 15, of which waited for: 2 -> 7; matrix products, arithmetic and copies ran while one was open for 5% -> 16% of each run, Pallas kernels for 0% -> 0%
where the time goes in v1:
time: 737 us; the launch traced here: 730 us
  other arithmetic  297 us (40%)
  waiting for transfers between devices  137 us (19%)
  local copies, waits for them, and re-layouts  126 us (17%)
  matrix products  111 us (15%)
  starting transfers between devices  23 us (3%)
  loops' own time  19.2 us (3%)
  blocking collectives  15.7 us (2%)
    ppermute x12, waiting for transfers between devices, exchanged(): lax.ppermute(spectra, 'grp', [(i, i ^ hop) for i in range(groups)])  130 us
    concatenate x8, other arithmetic, add_chunk(): weights = jnp.concatenate([w_re, w_im], axis=3).astype(jnp.bfloat16)  60.7 us
    cos x16, other arithmetic, unit_circle(): return (jnp.cos(angles), jnp.sin(angles))  57.9 us
    add x8, other arithmetic, add_chunk(): y_im = products[:, :, 0, :, NS_FEEDS:] + products[:, :, 1, :, :NS_FEEDS]  51.5 us
    dot_general x16, matrix products, exchanged(): lax.dot_general(tables[hop], filtered, (((1,), (1,)), ((), ())), preferre...  47.7 us
    reshape x2, local copies, waits for them, and re-layouts, local(): jnp.stack(received)  40.1 us
    another operation x12, other arithmetic  39 us
    dot_general x8, matrix products, add_chunk(): lax.dot_general(rows, weights, (((2,), (1,)), ((0,), (0,))), preferred_el...  37.1 us
  transfers between devices with their start and end apart: 15, of which 7 were waited for; matrix products, arithmetic and copies ran while one was open for 16% of the time, Pallas kernels for 0%

profile of v1, /device:TPU:0, one launch (start us, length us, event | category | flops | bytes accessed | tf_op | source)
XLA Modules:
  0.0 730.0 jit_solution(13410717650484641341)
XLA Ops:
  2.3 6.3 all-to-all-start
  12.6 5.6 collective-permute-start
  22.1 21.4 %add_convert_fusion.1 = (bf16[4,256,2048]{2,1,0:T(8,128)(2,1)}, bf16[4,256,2048]{2,1,0:T(8,128)(2,1)S(1)}, bf16[4,256,2048]{2,1,0:T(8,128)(2,1)S(1)}) fusion(bf16[16,256,2048]{2,1,0:T(8,128)(2,1)} %param.6, f32[2048]{0:T(1024)S(1)} %get-tuple-element.508, f32[2048]{0:T(1024)S(1)} %get-tuple-element.509, f32[2048]{0:T(1024)S(1)} %get-tuple-element.510, ...), kind=kLoop, calls=%fused_computation.124 | loop fusion | flops 75497472 | bytes 62947328 | tf_op jit(solution)/shard_map/convert_element_type | solution.py:148
  90.1 4.8 slice.585
  97.6 8.4 %add_convert_fusion.4 = bf16[4,256,2048]{2,1,0:T(8,128)(2,1)S(1)} fusion(bf16[4,256,2048]{2,1,0:T(8,128)(2,1)} %slice.585, bf16[3,256,2048]{2,1,0:T(8,128)(2,1)} %collective-permute-done, f32[2048]{0:T(1024)S(1)} %get-tuple-element.508, f32[2048]{0:T(1024)S(1)} %get-tuple-element.509, f32[2048]{0:T(1024)S(1)} %get-tuple-element.510, ...), kind=kLoop, calls=%fused_computation.127 | loop fusion | flops 31457280 | bytes 11567104 | tf_op jit(solution)/shard_map/convert_element_type | solution.py:148
  120.2 16.7 %collective-permute-done.2 = bf16[512,1024]{1,0:T(8,128)(2,1)S(1)} collective-permute-done((bf16[512,1024]{1,0:T(8,128)(2,1)S(1)}, bf16[512,1024]{1,0:T(8,128)(2,1)S(1)}, u32[]{:S(2)}, u32[]{:S(2)}) %collective-permute-start.2) | collective-permute-done | bytes 1048608 | tf_op jit(solution)/shard_map/ppermute | solution.py:156
  138.5 42.5 %collective-permute-done.3 = bf16[512,1024]{1,0:T(8,128)(2,1)S(1)} collective-permute-done((bf16[512,1024]{1,0:T(8,128)(2,1)S(1)}, bf16[512,1024]{1,0:T(8,128)(2,1)S(1)}, u32[]{:S(2)}, u32[]{:S(2)}) %collective-permute-start.3) | collective-permute-done | bytes 1048608 | tf_op jit(solution)/shard_map/ppermute | solution.py:156
  194.8 9.5 %collective-permute-done.8 = bf16[512,1024]{1,0:T(8,128)(2,1)S(1)} collective-permute-done((bf16[512,1024]{1,0:T(8,128)(2,1)S(1)}, bf16[512,1024]{1,0:T(8,128)(2,1)S(1)}, u32[]{:S(2)}, u32[]{:S(2)}) %collective-permute-start.8) | collective-permute-done | bytes 1048608 | tf_op jit(solution)/shard_map/ppermute | solution.py:156
  205.4 20.6 %collective-permute-done.9 = bf16[512,1024]{1,0:T(8,128)(2,1)S(1)} collective-permute-done((bf16[512,1024]{1,0:T(8,128)(2,1)S(1)}, bf16[512,1024]{1,0:T(8,128)(2,1)S(1)}, u32[]{:S(2)}, u32[]{:S(2)}) %collective-permute-start.9) | collective-permute-done | bytes 1048608 | tf_op jit(solution)/shard_map/ppermute | solution.py:156
  229.2 20.1 %collective-permute-done.11 = bf16[512,1024]{1,0:T(8,128)(2,1)S(1)} collective-permute-done((bf16[512,1024]{1,0:T(8,128)(2,1)S(1)}, bf16[512,1024]{1,0:T(8,128)(2,1)S(1)}, u32[]{:S(2)}, u32[]{:S(2)}) %collective-permute-start.11) | collective-permute-done | bytes 1048608 | tf_op jit(solution)/shard_map/ppermute | solution.py:156
  250.4 20.6 %collective-permute-done.12 = bf16[512,1024]{1,0:T(8,128)(2,1)S(1)} collective-permute-done((bf16[512,1024]{1,0:T(8,128)(2,1)S(1)}, bf16[512,1024]{1,0:T(8,128)(2,1)S(1)}, u32[]{:S(2)}, u32[]{:S(2)}) %collective-permute-start.12) | collective-permute-done | bytes 1048608 | tf_op jit(solution)/shard_map/ppermute | solution.py:156
  272.0 27.9 %reshape.349 = bf16[4,4,2,256,4,256]{5,4,3,2,1,0:T(4,128)(2,1)} reshape(bf16[16,2,256,1024]{3,2,1,0:T(8,128)(2,1)} %constant_dynamic-update-slice_fusion) | data formatting | bytes 33554432 | tf_op jit(solution)/shard_map/reshape | solution.py:178
  299.9 12.2 %copy.70 = bf16[4,4,2,256,4,256]{5,4,0,2,1,3:T(4,128)(2,1)} copy(bf16[4,4,2,256,4,256]{5,4,3,2,1,0:T(4,128)(2,1)} %reshape.349) | data formatting | bytes 33554432 | tf_op jit(solution)/shard_map/reshape | solution.py:178
  312.0 23.7 %reshape.350 = bf16[256,4,2,16,256]{4,3,2,1,0:T(8,128)(2,1)} reshape(bf16[256,4,2,4,4,256]{5,4,3,2,1,0:T(4,128)(2,1)} %bitcast.342) | data formatting | bytes 33554432 | tf_op jit(solution)/shard_map/reshape | solution.py:181
  335.7 351.7 %while.20 = (s32[]{:T(128)}, f32[4,16,1024]{2,0,1:T(4,128)S(1)}, f32[256,4]{0,1:T(4,128)S(1)}, bf16[256,4,2,16,256]{4,3,2,1,0:T(8,128)(2,1)}, s32[]{:T(128)}, /*...) while((s32[]{:T(128)}, f32[4,16,1024]{2,0,1:T(4,128)S(1)}, ...), condition=%wide.region_2.3_spmd.clone.clone.clone.clone, body=%wide.region_1.2_spmd.clone.clone.clone.clone.sunk | while | flops 1162548480 | bytes 112474704 | solution.py:95
  359.7 7.1 fusion.195
  371.4 7.6 %pad_maximum_fusion.7 = bf16[32,256,512]{2,1,0:T(8,128)(2,1)} fusion(bf16[32,256,256]{2,1,0:T(8,128)(2,1)} %bitcast.340, bf16[32,256,256]{2,1,0:T(8,128)(2,1)} %bitcast.339), kind=kLoop, calls=%fused_computation.4.clone.1 | loop fusion | flops 16777216 | bytes 16777216 | tf_op jit(solution)/shard_map/while/body/eval_jaxpr/concatenate | solution.py:69
  379.0 4.6 fusion.197
  384.9 6.4 fusion.199
  401.4 7.1 fusion.195
  413.1 7.6 %pad_maximum_fusion.7 = bf16[32,256,512]{2,1,0:T(8,128)(2,1)} fusion(bf16[32,256,256]{2,1,0:T(8,128)(2,1)} %bitcast.340, bf16[32,256,256]{2,1,0:T(8,128)(2,1)} %bitcast.339), kind=kLoop, calls=%fused_computation.4.clone.1 | loop fusion | flops 16777216 | bytes 16777216 | tf_op jit(solution)/shard_map/while/body/eval_jaxpr/concatenate | solution.py:69
  420.7 4.6 fusion.197
  426.7 6.4 fusion.199
  443.2 7.1 fusion.195
  454.8 7.6 %pad_maximum_fusion.7 = bf16[32,256,512]{2,1,0:T(8,128)(2,1)} fusion(bf16[32,256,256]{2,1,0:T(8,128)(2,1)} %bitcast.340, bf16[32,256,256]{2,1,0:T(8,128)(2,1)} %bitcast.339), kind=kLoop, calls=%fused_computation.4.clone.1 | loop fusion | flops 16777216 | bytes 16777216 | tf_op jit(solution)/shard_map/while/body/eval_jaxpr/concatenate | solution.py:69
  468.4 6.4 fusion.199
  484.9 7.1 fusion.195
  496.6 7.6 %pad_maximum_fusion.7 = bf16[32,256,512]{2,1,0:T(8,128)(2,1)} fusion(bf16[32,256,256]{2,1,0:T(8,128)(2,1)} %bitcast.340, bf16[32,256,256]{2,1,0:T(8,128)(2,1)} %bitcast.339), kind=kLoop, calls=%fused_computation.4.clone.1 | loop fusion | flops 16777216 | bytes 16777216 | tf_op jit(solution)/shard_map/while/body/eval_jaxpr/concatenate | solution.py:69
  510.1 6.4 fusion.199
  526.6 7.1 fusion.195
  538.3 7.6 %pad_maximum_fusion.7 = bf16[32,256,512]{2,1,0:T(8,128)(2,1)} fusion(bf16[32,256,256]{2,1,0:T(8,128)(2,1)} %bitcast.340, bf16[32,256,256]{2,1,0:T(8,128)(2,1)} %bitcast.339), kind=kLoop, calls=%fused_computation.4.clone.1 | loop fusion | flops 16777216 | bytes 16777216 | tf_op jit(solution)/shard_map/while/body/eval_jaxpr/concatenate | solution.py:69
  545.9 4.6 fusion.197
  551.8 6.4 fusion.199
  568.4 7.1 fusion.195
  580.0 7.6 %pad_maximum_fusion.7 = bf16[32,256,512]{2,1,0:T(8,128)(2,1)} fusion(bf16[32,256,256]{2,1,0:T(8,128)(2,1)} %bitcast.340, bf16[32,256,256]{2,1,0:T(8,128)(2,1)} %bitcast.339), kind=kLoop, calls=%fused_computation.4.clone.1 | loop fusion | flops 16777216 | bytes 16777216 | tf_op jit(solution)/shard_map/while/body/eval_jaxpr/concatenate | solution.py:69
  587.6 4.6 fusion.197
  593.6 6.4 fusion.199
  610.1 7.1 fusion.195
  621.7 7.6 %pad_maximum_fusion.7 = bf16[32,256,512]{2,1,0:T(8,128)(2,1)} fusion(bf16[32,256,256]{2,1,0:T(8,128)(2,1)} %bitcast.340, bf16[32,256,256]{2,1,0:T(8,128)(2,1)} %bitcast.339), kind=kLoop, calls=%fused_computation.4.clone.1 | loop fusion | flops 16777216 | bytes 16777216 | tf_op jit(solution)/shard_map/while/body/eval_jaxpr/concatenate | solution.py:69
  629.3 4.6 fusion.197
  635.3 6.4 fusion.199
  651.8 7.1 fusion.195
  663.5 7.6 %pad_maximum_fusion.7 = bf16[32,256,512]{2,1,0:T(8,128)(2,1)} fusion(bf16[32,256,256]{2,1,0:T(8,128)(2,1)} %bitcast.340, bf16[32,256,256]{2,1,0:T(8,128)(2,1)} %bitcast.339), kind=kLoop, calls=%fused_computation.4.clone.1 | loop fusion | flops 16777216 | bytes 16777216 | tf_op jit(solution)/shard_map/while/body/eval_jaxpr/concatenate | solution.py:69
  671.0 4.6 fusion.197
  677.0 6.4 fusion.199
  693.8 6.6 all-to-all-done.1
  700.4 15.7 %all_gather.3 = f32[64,16,128]{2,1,0:T(8,128)S(1)} all-gather(f32[16,16,128]{2,1,0:T(8,128)S(1)} %bitcast.385), channel_id=1, replica_groups=mesh['grp'=8,'band'=4] {'band'}, dimensions={0}, use_global_device_ids=true | all-gather | bytes 655360 | tf_op jit(solution)/shard_map/all_gather | solution.py:206
  716.3 13.3 %fusion.57 = f32[64,128,128]{2,1,0:T(8,128)} fusion(s32[16,64,128]{2,1,0:T(8,128)S(1)} %add_select_fusion.5, f32[16,64,128]{2,1,0:T(8,128)S(1)} %bitcast_subtract_fusion), kind=kOutput, calls=%fused_computation.134 | convolution fusion | flops 12894339072 | bytes 5242880 | tf_op jit(solution)/shard_map/smb,smtd->btd/dot_general | solution.py:104
  (320 shorter events, 236.5 us)
Async XLA Ops:
  2.3 92.5 %all-to-all-start = ((s32[4,1,768]{2,1,0:T(1,128)}), s32[4,1,768]{2,1,0:T(1,128)S(1)}, u32[]{:S(2)}, u32[]{:S(2)}) async-start(s32[4,1,768]{2,1,0:T(1,128)} %copy.43), calls=%async_computation | async-start | bytes 24576 | tf_op jit(solution)/shard_map/all_to_all | solution.py:130
  12.6 85.0 %collective-permute-start = (bf16[3,256,2048]{2,1,0:T(8,128)(2,1)}, bf16[3,256,2048]{2,1,0:T(8,128)(2,1)}, u32[]{:S(2)}, u32[]{:S(2)}) collective-permute-start(bf16[3,256,2048]{2,1,0:T(8,128)(2,1)} %slice.584), channel_id=1, source_target_pairs={{0,1},{1,2},{2,3},{4,5},{5,6},{6,7},{8,9},{9,10},{10,11},{12,13},{... | collective-permute-start | bytes 9437192 | tf_op jit(solution)/shard_map/ppermute | solution.py:23
  22.0 57.3 %copy-start.6 = (bf16[512,2048]{1,0:T(8,128)(2,1)}, bf16[512,2048]{1,0:T(8,128)(2,1)S(1)}, u32[]{:S(2)}) copy-start(bf16[512,2048]{1,0:T(8,128)(2,1)S(1)} %pad_maximum_fusion.3) | copy-start | bytes 6291460
  43.4 3.7 copy-start
  43.4 3.7 copy-start.3
  47.1 66.7 %collective-permute-start.7 = (bf16[512,1024]{1,0:T(8,128)(2,1)}, bf16[512,1024]{1,0:T(8,128)(2,1)}, u32[]{:S(2)}, u32[]{:S(2)}) collective-permute-start(bf16[512,1024]{1,0:T(8,128)(2,1)} %convolution_convert_fusion.6), channel_id=1, source_target_pairs={{0,4},{4,0},{8,12},{12,8},{16,20},{20,16},{24,28},{28,24},{1,5},{5... | collective-permute-start | bytes 3145736 | tf_op jit(solution)/shard_map/ppermute | solution.py:156
  50.5 133.4 %collective-permute-start.4 = (bf16[512,1024]{1,0:T(8,128)(2,1)}, bf16[512,1024]{1,0:T(8,128)(2,1)}, u32[]{:S(2)}, u32[]{:S(2)}) collective-permute-start(bf16[512,1024]{1,0:T(8,128)(2,1)} %convolution_convert_fusion.10), channel_id=1, source_target_pairs={{0,4},{4,0},{8,12},{12,8},{16,20},{20,16},{24,28},{28,24},{1,5},{5... | collective-permute-start | bytes 3145736 | tf_op jit(solution)/shard_map/ppermute | solution.py:156
  51.1 2.2 copy-start.4
  53.2 3.3 copy-start.8
  56.6 129.6 %collective-permute-start.5 = (bf16[512,1024]{1,0:T(8,128)(2,1)}, bf16[512,1024]{1,0:T(8,128)(2,1)}, u32[]{:S(2)}, u32[]{:S(2)}) collective-permute-start(bf16[512,1024]{1,0:T(8,128)(2,1)} %convolution_convert_fusion.9), channel_id=1, source_target_pairs={{0,8},{4,12},{8,0},{12,4},{16,24},{20,28},{24,16},{28,20},{1,9},{5... | collective-permute-start | bytes 3145736 | tf_op jit(solution)/shard_map/ppermute | solution.py:156
  58.1 2.2 copy-start.5
  60.3 7.1 copy-start.11
  60.3 3.4 copy-start.1
  63.6 3.8 copy-start.2
  67.4 3.4 copy-start.9
  74.1 3.4 copy-start.17
  79.4 8.3 %copy-start.13 = (bf16[512,2048]{1,0:T(8,128)(2,1)}, bf16[512,2048]{1,0:T(8,128)(2,1)S(1)}, u32[]{:S(2)}) copy-start(bf16[512,2048]{1,0:T(8,128)(2,1)S(1)} %pad_maximum_fusion.2) | copy-start | bytes 6291460
  97.6 8.4 %copy-start.7 = (bf16[512,2048]{1,0:T(8,128)(2,1)S(1)}, bf16[512,2048]{1,0:T(8,128)(2,1)}, u32[]{:S(2)}) copy-start(bf16[512,2048]{1,0:T(8,128)(2,1)} %copy-done.6) | copy-start | bytes 6291460
  106.0 2.5 copy-start.10
  108.4 3.1 copy-start.12
  108.4 6.8 collective-permute-start.1
  110.9 3.0 copy-start.24
  110.9 4.8 copy-start.14
  110.9 26.0 %collective-permute-start.2 = (bf16[512,1024]{1,0:T(8,128)(2,1)S(1)}, bf16[512,1024]{1,0:T(8,128)(2,1)S(1)}, u32[]{:S(2)}, u32[]{:S(2)}) collective-permute-start(bf16[512,1024]{1,0:T(8,128)(2,1)S(1)} %convolution_convert_fusion.13), channel_id=1, source_target_pairs={{0,8},{4,12},{8,0},{12,4},{16,24},{20,28},{24,16},{28,20},{1,9},{5... | collective-permute-start | bytes 3145736 | tf_op jit(solution)/shard_map/ppermute | solution.py:156
  113.9 76.1 %collective-permute-start.6 = (bf16[512,1024]{1,0:T(8,128)(2,1)S(1)}, bf16[512,1024]{1,0:T(8,128)(2,1)S(1)}, u32[]{:S(2)}, u32[]{:S(2)}) collective-permute-start(bf16[512,1024]{1,0:T(8,128)(2,1)S(1)} %copy-done.24), channel_id=1, source_target_pairs={{0,12},{4,8},{8,4},{12,0},{16,28},{20,24},{24,20},{28,16},{1,13},{... | collective-permute-start | bytes 3145736 | tf_op jit(solution)/shard_map/ppermute | solution.py:156
  115.3 65.8 %collective-permute-start.3 = (bf16[512,1024]{1,0:T(8,128)(2,1)S(1)}, bf16[512,1024]{1,0:T(8,128)(2,1)S(1)}, u32[]{:S(2)}, u32[]{:S(2)}) collective-permute-start(bf16[512,1024]{1,0:T(8,128)(2,1)S(1)} %convolution_convert_fusion.12), channel_id=1, source_target_pairs={{0,12},{4,8},{8,4},{12,0},{16,28},{20,24},{24,20},{28,16},{1,13},{... | collective-permute-start | bytes 3145736 | tf_op jit(solution)/shard_map/ppermute | solution.py:156
  118.1 18.8 %copy-start.22 = (bf16[512,1024]{1,0:T(8,128)(2,1)S(1)}, bf16[512,1024]{1,0:T(8,128)(2,1)}, u32[]{:S(2)}) copy-start(bf16[512,1024]{1,0:T(8,128)(2,1)} %convolution_convert_fusion.5) | copy-start | bytes 3145732
  118.1 63.0 %copy-start.21 = (bf16[512,1024]{1,0:T(8,128)(2,1)S(1)}, bf16[512,1024]{1,0:T(8,128)(2,1)}, u32[]{:S(2)}) copy-start(bf16[512,1024]{1,0:T(8,128)(2,1)} %convolution_convert_fusion.4) | copy-start | bytes 3145732
  119.2 64.7 %copy-start.23 = (bf16[512,1024]{1,0:T(8,128)(2,1)S(1)}, bf16[512,1024]{1,0:T(8,128)(2,1)}, u32[]{:S(2)}) copy-start(bf16[512,1024]{1,0:T(8,128)(2,1)} %convolution_convert_fusion.2) | copy-start | bytes 3145732
  136.9 67.4 %collective-permute-start.8 = (bf16[512,1024]{1,0:T(8,128)(2,1)S(1)}, bf16[512,1024]{1,0:T(8,128)(2,1)S(1)}, u32[]{:S(2)}, u32[]{:S(2)}) collective-permute-start(bf16[512,1024]{1,0:T(8,128)(2,1)S(1)} %copy-done.22), channel_id=1, source_target_pairs={{0,8},{4,12},{8,0},{12,4},{16,24},{20,28},{24,16},{28,20},{1,9},{5... | collective-permute-start | bytes 3145736 | tf_op jit(solution)/shard_map/ppermute | solution.py:156
  137.5 48.8 %copy-start.20 = (bf16[512,1024]{1,0:T(8,128)(2,1)S(1)}, bf16[512,1024]{1,0:T(8,128)(2,1)}, u32[]{:S(2)}) copy-start(bf16[512,1024]{1,0:T(8,128)(2,1)} %convolution_convert_fusion.1) | copy-start | bytes 3145732
  181.0 44.9 %collective-permute-start.9 = (bf16[512,1024]{1,0:T(8,128)(2,1)S(1)}, bf16[512,1024]{1,0:T(8,128)(2,1)S(1)}, u32[]{:S(2)}, u32[]{:S(2)}) collective-permute-start(bf16[512,1024]{1,0:T(8,128)(2,1)S(1)} %copy-done.21), channel_id=1, source_target_pairs={{0,12},{4,8},{8,4},{12,0},{16,28},{20,24},{24,20},{28,16},{1,13},{... | collective-permute-start | bytes 3145736 | tf_op jit(solution)/shard_map/ppermute | solution.py:156
  181.8 8.2 %copy-start.19 = (bf16[512,1024]{1,0:T(8,128)(2,1)S(1)}, bf16[512,1024]{1,0:T(8,128)(2,1)}, u32[]{:S(2)}) copy-start(bf16[512,1024]{1,0:T(8,128)(2,1)} %convolution_convert_fusion) | copy-start | bytes 3145732
  183.9 44.2 %collective-permute-start.10 = (bf16[512,1024]{1,0:T(8,128)(2,1)S(1)}, bf16[512,1024]{1,0:T(8,128)(2,1)S(1)}, u32[]{:S(2)}, u32[]{:S(2)}) collective-permute-start(bf16[512,1024]{1,0:T(8,128)(2,1)S(1)} %copy-done.23), channel_id=1, source_target_pairs={{0,4},{4,0},{8,12},{12,8},{16,20},{20,16},{24,28},{28,24},{1,5},{5... | collective-permute-start | bytes 3145736 | tf_op jit(solution)/shard_map/ppermute | solution.py:156
  186.2 63.0 %collective-permute-start.11 = (bf16[512,1024]{1,0:T(8,128)(2,1)S(1)}, bf16[512,1024]{1,0:T(8,128)(2,1)S(1)}, u32[]{:S(2)}, u32[]{:S(2)}) collective-permute-start(bf16[512,1024]{1,0:T(8,128)(2,1)S(1)} %copy-done.20), channel_id=1, source_target_pairs={{0,8},{4,12},{8,0},{12,4},{16,24},{20,28},{24,16},{28,20},{1,9},{5... | collective-permute-start | bytes 3145736 | tf_op jit(solution)/shard_map/ppermute | solution.py:156
  190.0 80.9 %collective-permute-start.12 = (bf16[512,1024]{1,0:T(8,128)(2,1)S(1)}, bf16[512,1024]{1,0:T(8,128)(2,1)S(1)}, u32[]{:S(2)}, u32[]{:S(2)}) collective-permute-start(bf16[512,1024]{1,0:T(8,128)(2,1)S(1)} %copy-done.19), channel_id=1, source_target_pairs={{0,12},{4,8},{8,4},{12,0},{16,28},{20,24},{24,20},{28,16},{1,13},{... | collective-permute-start | bytes 3145736 | tf_op jit(solution)/shard_map/ppermute | solution.py:156
  312.0 23.7 %copy-start.15 = (f32[4,16,1024]{2,0,1:T(4,128)S(1)}, f32[4,16,1024]{2,0,1:T(4,128)}, u32[]{:S(2)}) copy-start(f32[4,16,1024]{2,0,1:T(4,128)} %custom-call) | copy-start | bytes 786436
  335.7 351.9 %copy-start.18 = (s32[1,1024]{1,0:T(1,128)S(1)}, s32[1,1024]{1,0:T(1,128)}, u32[]{:S(2)}) copy-start(s32[1,1024]{1,0:T(1,128)} %slice_add_fusion) | copy-start | bytes 12292
  335.7 357.8 %copy-start.16 = (s32[128,4,4]{0,2,1:T(4,128)S(1)}, s32[128,4,4]{0,2,1:T(4,128)}, u32[]{:S(2)}) copy-start(s32[128,4,4]{0,2,1:T(4,128)} %copy.50) | copy-start | bytes 24580
  690.1 10.3 %all-to-all-start.1 = ((f32[1,4,16,8,128]{4,2,1,0,3:T(8,128)}), f32[1,4,16,8,128]{4,2,1,0,3:T(8,128)S(1)}, u32[]{:S(2)}, u32[]{:S(2)}) async-start(f32[1,4,16,8,128]{4,2,1,0,3:T(8,128)} %copy.46), calls=%async_computation.1 | async-start | bytes 524288 | tf_op jit(solution)/shard_map/all_to_all | solution.py:194
